TPU v7x, 512 devices: a whole 4x8x8 slice. The times are simulated.
512 devices in a mesh: role: 4 (over x), cls: 128 (over y, z, core).
Axes of the slice: x: 4, y: 8, z: 8, core: 2. Of those that a mesh axis runs over, the one named last changes fastest.
Arguments:
- features: bfloat16 [1024, 512], P('cls', 'role'), may hold values from -160 to 160, as said below
- centres: bfloat16 [1572864, 512], P(('role', 'cls')), may hold values from -0.25 to 0.25
- samples: int32 [512, 1024], P(('role', 'cls')), may hold values from 0 to 3071, as said below
- counts: int32 [512], P(('role', 'cls')), may hold values from 64 to 1024, as said below
- label_row: int32 [1024], replicated, may hold values from 0 to 3071, as said below
- owner: int32 [1024], replicated, may hold values from 0 to 511, as said below
Outputs:
- feature_grad: float32 [1024, 512], P('cls', 'role')
- centre_grad: bfloat16 [512, 1024, 512], P(('role', 'cls'))
- loss: float32 [1024], P('cls')
Inputs may be any that keep to these rules, and one draw needn't show every extreme that they name: `features`: scaled values with spread per image and per feature. `samples`: entries of one shard are distinct; only the first counts[q] entries of shard q are used. `counts`: each count is 1024 divided by 1, 2, 4, 8 or 16; some shard has exactly 1024. label_row[i] stands among the first counts[owner[i]] entries of samples[owner[i]]. `owner`: index of the owning shard along role+cls; shards with more used slots own more images.
All inputs are finite; a program needn't handle non-finite values.
Results may differ from a plain program's by a relative error of at most 0.0061.
Values may be sent and summed in bfloat16 or wider, within the bound.
A program may use at most 64 MiB of HBM per device.

v0:
```python
import math

import jax
import jax.numpy as jnp
from jax import lax
from jax.sharding import PartitionSpec as P

logit_scale = 64.0
margin_cos = math.cos(0.5)
margin_sin = math.sin(0.5)
epsilon = 1e-05


def body(features, centres, samples, counts, label_row, owner):
    cls_size = lax.axis_size("cls")
    img_rows = features.shape[0]
    images = img_rows * cls_size
    values = features.astype(jnp.float32)
    col_mean = lax.psum(jnp.sum(values, 0), "cls") / images
    centred = values - col_mean
    col_var = lax.psum(jnp.sum(centred * centred, 0), "cls") / images
    inv_std = lax.rsqrt(col_var + epsilon)
    normed = centred * inv_std
    norm_sq = lax.psum(jnp.sum(normed * normed, 1), "role")
    inv_norm = lax.rsqrt(norm_sq + epsilon)
    unit_feats = normed * inv_norm[:, None]
    widened = lax.all_gather(unit_feats.astype(jnp.bfloat16), "role", axis=1, tiled=True)
    gathered = lax.all_gather(widened, "cls", axis=0, tiled=True)
    shard_id = lax.axis_index("role") * cls_size + lax.axis_index("cls")
    row_ids = samples[0]
    live_count = counts[0]
    picked = jnp.take(centres, row_ids, axis=0).astype(jnp.float32)
    w_inv = lax.rsqrt(jnp.sum(picked * picked, 1) + epsilon)
    w_unit = picked * w_inv[:, None]
    w_round = w_unit.astype(jnp.bfloat16)
    cosine = lax.dot_general(
        gathered, w_round, (((1,), (1,)), ((), ())), preferred_element_type=jnp.float32
    )
    slot_ids = jnp.arange(row_ids.shape[0], dtype=jnp.int32)
    usable = slot_ids < live_count
    positive = (
        (owner[:, None] == shard_id) & (label_row[:, None] == row_ids[None, :]) & usable[None, :]
    )
    sine_part = jnp.sqrt(jnp.maximum(1.0 - cosine * cosine, 0.0))
    target = cosine * margin_cos - sine_part * margin_sin
    logits = logit_scale * jnp.where(positive, target, cosine)
    exp_terms = jnp.where(usable[None, :], jnp.exp(logits), jnp.float32(0.0))
    part_sum = jnp.sum(exp_terms, 1)
    part_pos = jnp.sum(jnp.where(positive, logits, jnp.float32(0.0)), 1)
    partition_sum, positive_logit = lax.psum((part_sum, part_pos), ("role", "cls"))
    loss_all = jnp.log(partition_sum) - positive_logit
    loss = lax.dynamic_slice_in_dim(loss_all, lax.axis_index("cls") * img_rows, img_rows, 0)
    grad_logit = logit_scale * (exp_terms / partition_sum[:, None] - positive.astype(jnp.float32))
    grad_round = grad_logit.astype(jnp.bfloat16)
    back_rows = lax.dot_general(
        grad_round, gathered, (((0,), (0,)), ((), ())), preferred_element_type=jnp.float32
    )
    radial_rows = jnp.sum(w_unit * back_rows, 1, keepdims=True)
    centre_grad = ((back_rows - w_unit * radial_rows) * w_inv[:, None]).astype(jnp.bfloat16)[None]
    full_grad = jnp.dot(grad_round, w_round, preferred_element_type=jnp.float32)
    split_grad = lax.psum_scatter(full_grad, "role", scatter_dimension=1, tiled=True)
    grad_unit = lax.psum_scatter(split_grad, "cls", scatter_dimension=0, tiled=True)
    radial_part = lax.psum(jnp.sum(unit_feats * grad_unit, 1), "role")
    grad_normed = (grad_unit - unit_feats * radial_part[:, None]) * inv_norm[:, None]
    grad_total, cross_total = lax.psum(
        (jnp.sum(grad_normed, 0), jnp.sum(grad_normed * normed, 0)), "cls"
    )
    feature_grad = (grad_normed - grad_total / images - normed * (cross_total / images)) * inv_std
    return (feature_grad, centre_grad, loss)


def solution(mesh):
    return jax.shard_map(
        body,
        mesh=mesh,
        in_specs=(
            P("cls", "role"),
            P(("role", "cls"), None),
            P(("role", "cls"), None),
            P(("role", "cls")),
            P(),
            P(),
        ),
        out_specs=(P("cls", "role"), P(("role", "cls"), None, None), P("cls")),
        check_vma=False,
    )
```

profile of v0, /device:TPU:1, one launch (start us, length us, event | category | flops | bytes accessed | tf_op | source)
XLA Modules:
  0.0 1212.5 jit_solution(9806286267377754459)
XLA Ops:
  7.2 0.8 convert_reduce_fusion
  8.1 254.6 %psum.56 = f32[128]{0:T(128)S(1)} all-reduce(f32[128]{0:T(128)S(1)} %convert_reduce_fusion), channel_id=1, replica_groups=mesh['role'=4,'cls'=128] {'cls'}, use_global_device_ids=true, to_apply=%region_1.0 | all-reduce | flops 128 | bytes 1024 | tf_op jit(solution)/shard_map/psum | solution.py:19
  262.7 0.7 fusion.31
  263.4 251.2 %psum.57 = f32[128]{0:T(128)S(1)} all-reduce(f32[128]{0:T(128)S(1)} %fusion.31), channel_id=1, replica_groups=mesh['role'=4,'cls'=128] {'cls'}, use_global_device_ids=true, to_apply=%region_3.0 | all-reduce | flops 128 | bytes 1024 | tf_op jit(solution)/shard_map/psum | solution.py:21
  514.6 0.8 fusion.27
  515.4 8.5 psum.58
  523.9 0.8 fusion.23
  524.6 8.4 all_gather.6
  533.1 0.0 reduce-scatter.2.cloned.1.call-start
  533.1 0.7 compare_select_fusion
  533.9 5.1 gather_fusion
  539.0 2.3 copy.13
  542.0 1.5 fusion.8
  543.5 66.5 %all-gather.2.cloned.1.call-done = bf16[1024,512]{1,0:T(8,128)(2,1)} async-done(((bf16[8,512]{1,0:T(8,128)(2,1)}), bf16[1024,512]{1,0:T(8,128)(2,1)}) %all-gather.2.cloned.1.call-update) | async-done | bytes 1048592 | tf_op jit(solution)/shard_map/all_gather | solution.py:28
  610.0 7.4 select_reduce_fusion
  617.4 96.5 %all-reduce.1 = (f32[1024]{0:T(1024)S(1)}, f32[1024]{0:T(1024)S(1)}) all-reduce(f32[1024]{0:T(1024)S(1)} %get-tuple-element.13, f32[1024]{0:T(1024)S(1)} %get-tuple-element.12), channel_id=1, replica_groups=mesh['role'=4,'cls'=128] {'role','cls'}, use_global_device_ids=true, to_apply=%region_8.9 | all-reduce | flops 2048 | bytes 16384 | tf_op jit(solution)/shard_map/psum | solution.py:50
  713.9 3.5 multiply_convert_fusion
  717.4 1.3 copy-done.2
  718.8 2.6 fusion.10
  721.4 0.0 all-reduce.5.cloned.1.call-start
  721.4 1.3 dynamic-slice
  723.4 4.8 fusion.4
  728.2 22.0 %reduce-scatter.2.cloned.1.call-done = f32[1024,128]{1,0:T(8,128)} async-done(((f32[1024,512]{1,0:T(8,128)}), f32[1024,128]{1,0:T(8,128)}) %reduce-scatter.2.cloned.1.call-update) | async-done | bytes 524304 | tf_op jit(solution)/shard_map/reduce_scatter | solution.py:61
  750.2 3.3 fusion.9
  753.5 2.3 copy.14
  755.8 188.5 %all-reduce.5.cloned.1.call-done = f32[1024,128]{1,0:T(8,128)} async-done(((f32[1024,128]{1,0:T(8,128)}), f32[1024,128]{1,0:T(8,128)}) %all-reduce.5.cloned.1.call-update) | async-done | bytes 524304
  944.3 0.9 fusion.24
  945.2 0.6 dynamic_slice.3
  945.8 8.4 psum.60
  954.1 0.8 fusion.34
  954.9 249.7 %all-reduce.2 = (f32[128]{0:T(128)S(1)}, f32[128]{0:T(128)S(1)}) all-reduce(f32[128]{0:T(128)S(1)} %get-tuple-element.15, f32[128]{0:T(128)S(1)} %get-tuple-element.14), channel_id=1, replica_groups=mesh['role'=4,'cls'=128] {'cls'}, use_global_device_ids=true, to_apply=%region_16.17 | all-reduce | flops 256 | bytes 2048 | tf_op jit(solution)/shard_map/psum | solution.py:65
  1204.6 1.4 fusion.30
  (27 shorter events, 0.2 us)
Async XLA Ops:
  7.2 526.7 %copy-start = (bf16[3072,512]{1,0:T(8,128)(2,1)S(1)}, bf16[3072,512]{1,0:T(8,128)(2,1)}, u32[]{:S(2)}) copy-start(bf16[3072,512]{1,0:T(8,128)(2,1)} %param.7) | copy-start | bytes 9437188
  7.2 602.8 %all-gather.2.cloned.1.call-start = ((), (), s32[]{:S(2)}) async-start(), calls=%async_computation.1 | async-start | bytes 1056768 | tf_op jit(solution)/shard_map/all_gather | solution.py:28
  533.1 217.1 %reduce-scatter.2.cloned.1.call-start = ((), (), s32[]{:S(2)}) async-start(), calls=%async_computation.2 | async-start | bytes 2621440 | tf_op jit(solution)/shard_map/reduce_scatter | solution.py:61
  533.8 8.1 copy-start.4
  533.9 8.1 copy-start.6
  539.0 71.0 %copy-start.5 = (s32[1024]{0:T(1024)S(1)}, s32[1024]{0:T(1024)}, u32[]{:S(2)}) copy-start(s32[1024]{0:T(1024)} %param.10) | copy-start | bytes 12292
  713.9 4.9 copy-start.1
  717.4 1.3 copy-start.2
  721.4 222.9 %all-reduce.5.cloned.1.call-start = ((), (), s32[]{:S(2)}) async-start(), calls=%async_computation.3 | async-start | bytes 1048576
  750.2 194.1 %copy-start.3 = (bf16[8,128]{1,0:T(8,128)(2,1)S(1)}, bf16[8,128]{1,0:T(8,128)(2,1)}, u32[]{:S(2)}) copy-start(bf16[8,128]{1,0:T(8,128)(2,1)} %param.6) | copy-start | bytes 6148
Sparse Core Ops, SparseCore 0:
  533.2 76.7 all-gather.1
  721.5 28.6 reduce-scatter.1
  753.7 190.5 all-reduce.4
where the time goes:
time: 1210 us
  blocking collectives  877 us (72%)
  waiting for transfers between devices  277 us (23%)
  other arithmetic  15.3 us (1%)
  between operations  15.2 us (1%)
  matrix products  14.8 us (1%)
  local copies, waits for them, and re-layouts  12.9 us (1%)
    psum x1, blocking collectives, body(): col_mean = lax.psum(jnp.sum(values, 0), 'cls') / images  255 us
    psum x1, blocking collectives, body(): col_var = lax.psum(jnp.sum(centred * centred, 0), 'cls') / images  251 us
    psum x1, blocking collectives, body(): lax.psum((jnp.sum(grad_normed, 0), jnp.sum(grad_normed * normed, 0)), 'cls')  250 us
    unnamed x4, waiting for transfers between devices  189 us
    psum x1, blocking collectives, body(): lax.psum((part_sum, part_pos), ('role', 'cls'))  96.5 us
    all_gather x1, waiting for transfers between devices, body(): gathered = lax.all_gather(widened, 'cls', axis=0, tiled=True)  66.5 us
  transfers between devices with their start and end apart: 3, of which 3 were waited for; matrix products, arithmetic and copies ran while one was open for 2% of the time, Pallas kernels for 0%

commit v1 on v0

v1 whole, which is shorter than its diff:
```python
import functools
import math

import jax
import jax.numpy as jnp
from jax import lax
from jax.experimental import pallas as pl
from jax.experimental.pallas import tpu as pltpu
from jax.sharding import PartitionSpec as P

logit_scale = 64.0
margin_cos = math.cos(0.5)
margin_sin = math.sin(0.5)
epsilon = 1e-05

MESH = pl.DeviceIdType.MESH
f32 = jnp.float32
bf16 = jnp.bfloat16
L = 128
H = 256


def column(row):
    return jnp.transpose(jnp.broadcast_to(row, (L, L)))


def row_sum(block):
    return jnp.sum(jnp.transpose(block), axis=0, keepdims=True)


def margin_logit(cos):
    sine = jnp.sqrt(jnp.maximum(1.0 - cos * cos, 0.0))
    return logit_scale * (cos * margin_cos - sine * margin_sin)


def near_first(n):
    return sorted(range(1, n), key=lambda o: min(o, n - o))


def kernel(
    n, rows, images, slots, held,
    feat_ref, cen_hbm, samp_ref, count_ref, label_ref, owner_ref,
    fg_ref, cg_hbm, loss_ref,
    cen, picked, wround, wtrans, winv, labels, xbuf, feats, normed, inorm, ebuf, gbuf, qbuf,
    a_src, a_recv, pay, r1, r2, r3, fsend, drecv, csend, csum, crecv, bsrc, brecv, asrc, arecv, cgbuf,
    cen_sem, cg_sem, a_s, a_r, b_s, b_r, c_s, c_r, d_s, d_r, r1_s, r1_r, r2_s, r2_r, r3_s, r3_r,
    ds_s, ds_r, cs_s, cs_r, bs_s, bs_r, as_s, as_r,
):
    x = lax.axis_index("role")
    c = lax.axis_index("cls")
    k = c % 2
    t = c // 2
    y = t // n
    z = t % n
    a = y + (z - y) * k
    b = z + (y - z) * k
    step_a = 2 * n - (2 * n - 2) * k
    step_b = 2 + (2 * n - 2) * k
    other = c + 1 - 2 * k
    half = x // 2
    blocks = images // L
    ring = near_first(n)

    def along_a(o):
        return x, c + ((a + o) % n - a) * step_a

    def along_b(o):
        return x, c + ((b + o) % n - b) * step_b

    def remote(src, dst, send, recv, device):
        return pltpu.make_async_remote_copy(
            src_ref=src, dst_ref=dst, send_sem=send, recv_sem=recv, device_id=device, device_id_type=MESH
        )

    centre_copy = pltpu.make_async_copy(cen_hbm, cen, cen_sem)
    centre_copy.start()

    barrier = pltpu.get_barrier_semaphore()
    for o in range(1, n):
        for device in (along_a(o), along_b(o)):
            pl.semaphore_signal(barrier, inc=1, device_id=device, device_id_type=MESH)
    group = [((x + i // 2) % 4, c + (i % 2) * (1 - 2 * k)) for i in range(1, 8)]
    for device in group:
        pl.semaphore_signal(barrier, inc=1, device_id=device, device_id_type=MESH)
    a_src[...] = feat_ref[...].astype(f32)
    pl.semaphore_wait(barrier, 2 * (n - 1) + 7)

    def hop_one(i):
        return remote(
            a_src, a_recv.at[x % 2, k], a_s.at[i], a_r.at[(x % 2) * 2 + k], ((x + i) % 4, c - k + half)
        )

    for i in (1, 2, 3):
        hop_one(i).start()

    @pl.when(half != k)
    def _():
        hop_one(0).start()

    @pl.when(half == k)
    def _():
        a_recv[x % 2, k] = a_src[...]

    for j in range(2):
        for core in range(2):

            @pl.when(jnp.logical_or(2 * k + j != x, k != core))
            def _(j=j, core=core):
                remote(
                    a_src, a_recv.at[j, core], a_s.at[0], a_r.at[j * 2 + core], (x, other)
                ).wait_recv()

    tile = jnp.concatenate(
        [jnp.concatenate([a_recv[j, 0], a_recv[j, 1]], axis=0) for j in range(2)], axis=1
    )
    xbuf[k, y, z] = tile.astype(bf16)

    hop_two = {
        o: remote(xbuf.at[k, y, z], xbuf.at[k, y, z], b_s.at[o - 1], b_r.at[o - 1], along_a(o)) for o in ring
    }
    for o in ring:
        hop_two[o].start()

    shard = x * (2 * n * n) + c
    label_eff = jnp.where(owner_ref[...] == shard, label_ref[...], -1).astype(f32)
    for i in range(blocks):
        labels[i * L : (i + 1) * L, :] = column(label_eff[:, i * L : (i + 1) * L])
    slot = lax.broadcasted_iota(jnp.int32, (1, slots), 1)
    usable = slot < count_ref[0]
    slot_ids = jnp.where(usable, samp_ref[...], -2).astype(f32)
    slot_bias = jnp.where(usable, 0.0, -1e30).astype(f32)

    for o in ring:
        hop_two[o].wait_recv()

    def third(core):
        part = (lambda i: xbuf.at[0, :, i]) if core == 0 else (lambda i: xbuf.at[1, i])
        sends = {o: remote(part(b), part(b), c_s.at[o - 1], c_r.at[o - 1], along_b(o)) for o in ring}
        crosses = {
            o: remote(part((b - o) % n), part((b - o) % n), d_s.at[o], d_r.at[o], (x, other))
            for o in [0] + ring
        }
        return sends, crosses

    for core in range(2):

        @pl.when(k == core)
        def _(core=core):
            sends, crosses = third(core)
            for o in ring:
                sends[o].start()
            crosses[0].start()

    centre_copy.wait()
    lane = lax.broadcasted_iota(jnp.int32, (L, L), 1).astype(f32)

    def pick(i, carry):
        at = pl.ds(pl.multiple_of(i * L, L), L)
        ids = column(samp_ref[:, at].astype(f32))
        hot = [jnp.where(ids == lane + (j * L), 1.0, 0.0).astype(bf16) for j in range(held // L)]
        rows_f = jnp.dot(jnp.concatenate(hot, axis=1), cen[...], preferred_element_type=f32)
        picked[at, :] = rows_f.astype(bf16)
        inv = lax.rsqrt(jnp.sum(rows_f * rows_f, axis=1, keepdims=True) + epsilon)
        unit = rows_f * inv
        winv[at, :] = jnp.broadcast_to(inv, (L, L))
        wround[at, :] = unit.astype(bf16)
        wtrans[:, at] = jnp.transpose(unit).astype(bf16)
        return carry

    lax.fori_loop(0, slots // L, pick, 0)

    for core in range(2):

        @pl.when(k == core)
        def _(core=core):
            sends, crosses = third(core)
            for o in ring:
                sends[o].wait_recv()
                crosses[o].start()
            for o in [0] + ring:
                crosses[o].wait_recv()

    def part_of(h, i):
        return xbuf[h, i].reshape(n * rows, H).astype(f32)

    zero = jnp.zeros((1, H), f32)

    def add_up(i, sums):
        return tuple(sums[h] + jnp.sum(part_of(h, i), axis=0, keepdims=True) for h in range(2))

    mean = [s / images for s in lax.fori_loop(0, n, add_up, (zero, zero))]

    def add_squares(i, sums):
        out = []
        for h in range(2):
            centred = part_of(h, i) - mean[h]
            out.append(sums[h] + jnp.sum(centred * centred, axis=0, keepdims=True))
        return tuple(out)

    inv_std = [lax.rsqrt(s / images + epsilon) for s in lax.fori_loop(0, n, add_squares, (zero, zero))]

    m = n * rows

    def forward(i, carry):
        at = pl.ds(pl.multiple_of(i * m, m), m)
        norm = [(part_of(h, i) - mean[h]) * inv_std[h] for h in range(2)]
        squares = jnp.sum(norm[0] * norm[0], axis=1, keepdims=True) + jnp.sum(
            norm[1] * norm[1], axis=1, keepdims=True
        )
        inv = lax.rsqrt(squares + epsilon)
        inorm[at, :] = jnp.broadcast_to(inv, (m, L))
        unit = []
        for h in range(2):
            normed[h, at, :] = norm[h]
            unit.append((norm[h] * inv).astype(bf16))
        unit = jnp.concatenate(unit, axis=1)
        feats[at, :] = unit
        ebuf[at, :] = jnp.dot(unit, wtrans[...], preferred_element_type=f32)
        label = labels[at, :]
        cos_pos = jnp.zeros((m, L), f32)
        for j in range(slots // L):
            lanes = slice(j * L, (j + 1) * L)
            cos_pos += jnp.where(label == slot_ids[:, lanes], ebuf[at, lanes], 0.0)
        total = jnp.sum(cos_pos, axis=1, keepdims=True)
        pos_exp = jnp.broadcast_to(jnp.exp(margin_logit(total)), (m, L))
        sums = jnp.zeros((m, L), f32)
        for j in range(slots // L):
            lanes = slice(j * L, (j + 1) * L)
            plain = jnp.exp(logit_scale * ebuf[at, lanes] + slot_bias[:, lanes])
            term = jnp.where(label == slot_ids[:, lanes], pos_exp, plain)
            ebuf[at, lanes] = term
            sums += term
        pay[0:1, at] = row_sum(sums)
        pay[1:2, at] = row_sum(cos_pos)
        return carry

    lax.fori_loop(0, n, forward, 0)

    r1[a] = pay[...]
    stage = [remote(pay, r1.at[a], r1_s.at[o - 1], r1_r.at[o - 1], along_a(o)) for o in ring]
    for copy in stage:
        copy.start()
    for copy in stage:
        copy.wait()
    pay[...] = functools.reduce(lambda u, v: u + v, [r1[i] for i in range(n)])
    r2[b] = pay[...]
    stage = [remote(pay, r2.at[b], r2_s.at[o - 1], r2_r.at[o - 1], along_b(o)) for o in ring]
    for copy in stage:
        copy.start()
    for copy in stage:
        copy.wait()
    pay[...] = functools.reduce(lambda u, v: u + v, [r2[i] for i in range(n)])
    r3[x * 2 + k] = pay[...]
    stage = [remote(pay, r3.at[x * 2 + k], r3_s.at[i], r3_r.at[i], device) for i, device in enumerate(group)]
    for copy in stage:
        copy.start()
    for copy in stage:
        copy.wait()
    pay[...] = functools.reduce(lambda u, v: u + v, [r3[i] for i in range(8)])
    loss_ref[...] = jnp.log(pay[0:1, :]) - margin_logit(pay[1:2, :])
    pay[0:1, :] = logit_scale / pay[0:1, :]

    def backward(i, sums):
        at = pl.ds(pl.multiple_of(i * m, m), m)
        scale = jnp.transpose(jnp.broadcast_to(pay[0:1, at], (L, m)))
        label = labels[at, :]
        parts = []
        for j in range(slots // L):
            lanes = slice(j * L, (j + 1) * L)
            hit = jnp.where(label == slot_ids[:, lanes], logit_scale, 0.0)
            parts.append((ebuf[at, lanes] * scale - hit).astype(bf16))
        grad = jnp.concatenate(parts, axis=1)
        gbuf[at, :] = grad
        by_unit = jnp.dot(grad, wround[...], preferred_element_type=f32)
        by_unit = [by_unit[:, :H], by_unit[:, H:]]
        inv = inorm[at, :]
        inv = jnp.concatenate([inv, inv], axis=1)
        unit = [normed[h, at, :] * inv for h in range(2)]
        radial = jnp.sum(unit[0] * by_unit[0] + unit[1] * by_unit[1], axis=1, keepdims=True)
        out = []
        for h in range(2):
            q = (by_unit[h] - unit[h] * radial) * inv
            qbuf[h, i] = q.reshape(n, rows, H)
            out.append(sums[2 * h] + jnp.sum(q, axis=0, keepdims=True))
            out.append(sums[2 * h + 1] + jnp.sum(q * normed[h, at, :], axis=0, keepdims=True))
        return tuple(out)

    sums = lax.fori_loop(0, n, backward, (zero,) * 4)
    shift = [sums[0] / images, sums[2] / images]
    slope = [sums[1] / images, sums[3] / images]

    def pick_half(pair, mine):
        first = jnp.where(mine, k, 1 - k) == 0
        return jnp.where(first, pair[0], pair[1])

    def finish(h, i, mine):
        at = pl.ds(pl.multiple_of(i * m, m), m)
        q = qbuf[h, i].reshape(m, H)
        return (q - pick_half(shift, mine) - normed[h, at, :] * pick_half(slope, mine)) * pick_half(
            inv_std, mine
        )

    def theirs(i, carry):
        fsend[i] = finish(1 - k, i, False).reshape(n, rows, H).astype(bf16)
        return carry

    lax.fori_loop(0, n, theirs, 0)

    def reduce_hops(core):
        mine = (lambda i: drecv.at[:, i]) if core == 0 else (lambda i: drecv.at[i])
        cross_src = (lambda i: fsend.at[i]) if core == 0 else (lambda i: fsend.at[:, i])
        cross_dst = (lambda i: drecv.at[i]) if core == 0 else (lambda i: drecv.at[:, i])
        cross = [remote(cross_src(i), cross_dst(i), ds_s.at[i], ds_r.at[i], (x, other)) for i in range(n)]
        arrive = [remote(mine(i), mine(i), ds_s.at[i], ds_r.at[i], (x, other)) for i in range(n)]
        return cross, arrive

    for core in range(2):

        @pl.when(k == core)
        def _(core=core):
            for copy in reduce_hops(core)[0]:
                copy.start()

    def ours(i, carry):
        qbuf[k, i] = finish(k, i, True).reshape(n, rows, H)
        return carry

    lax.fori_loop(0, n, ours, 0)

    sends = {o: remote(csend.at[o - 1], crecv.at[o - 1], cs_s.at[o - 1], cs_r.at[o - 1], along_b(o)) for o in ring}
    for core in range(2):

        @pl.when(k == core)
        def _(core=core):
            for copy in reduce_hops(core)[1]:
                copy.wait_recv()

            def both(i):
                if core == 0:
                    return qbuf[0, :, i] + drecv[:, i].astype(f32)
                return qbuf[1, i] + drecv[i].astype(f32)

            for o in ring[::-1]:
                csend[o - 1] = both((b + o) % n).astype(bf16)
                sends[o].start()
            csum[...] = both(b)

    def by_centre(i, carry):
        at = pl.ds(pl.multiple_of(i * L, L), L)
        back = lax.dot_general(
            gbuf[:, at], feats[...], (((0,), (0,)), ((), ())), preferred_element_type=f32
        )
        inv = winv[at, :]
        inv = jnp.concatenate([inv] * (2 * H // L), axis=1)
        unit = picked[at, :].astype(f32) * inv
        radial = jnp.sum(unit * back, axis=1, keepdims=True)
        cgbuf[at, :] = ((back - unit * radial) * inv).astype(bf16)
        return carry

    lax.fori_loop(0, slots // L, by_centre, 0)
    out_copy = pltpu.make_async_copy(cgbuf, cg_hbm, cg_sem)
    out_copy.start()

    for o in ring:
        sends[o].wait_recv()
    for i in range(n):
        total = csum[i]
        for o in range(1, n):
            total += crecv[o - 1, i].astype(f32)
        bsrc[i] = total

    last = {
        o: remote(bsrc.at[(a + o) % n], brecv.at[o - 1], bs_s.at[o - 1], bs_r.at[o - 1], along_a(o)) for o in ring
    }
    for o in ring:
        last[o].start()
    for o in ring:
        last[o].wait_recv()
    total = bsrc[a]
    for o in range(1, n):
        total += brecv[o - 1]

    def hop_last(j, core):
        return remote(
            asrc.at[j, core], arecv.at[x], as_s.at[j * 2 + core], as_r.at[x], (2 * k + j, c - k + core)
        )

    for j in range(2):
        for core in range(2):
            asrc[j, core] = total[core * (rows // 2) : (core + 1) * (rows // 2), j * L : (j + 1) * L]
            mine = jnp.logical_and(2 * k + j == x, k == core)

            @pl.when(jnp.logical_not(mine))
            def _(j=j, core=core):
                hop_last(j, core).start()

            @pl.when(mine)
            def _(j=j, core=core):
                arecv[x] = asrc[j, core]

    for i in range(4):

        @pl.when(jnp.logical_or(x != i, half != k))
        def _(i=i):
            remote(asrc.at[0, 0], arecv.at[i], as_s.at[0], as_r.at[i], (x, other)).wait_recv()

    fg_ref[...] = (arecv[0] + arecv[1]) + (arecv[2] + arecv[3])

    for i in (1, 2, 3):
        hop_one(i).wait_send()

    @pl.when(half != k)
    def _():
        hop_one(0).wait_send()

    for o in ring:
        hop_two[o].wait_send()
        sends[o].wait_send()
        last[o].wait_send()
    for core in range(2):

        @pl.when(k == core)
        def _(core=core):
            first, crosses = third(core)
            for o in ring:
                first[o].wait_send()
            for o in [0] + ring:
                crosses[o].wait_send()
            for copy in reduce_hops(core)[0]:
                copy.wait_send()

    for j in range(2):
        for core in range(2):

            @pl.when(jnp.logical_or(2 * k + j != x, k != core))
            def _(j=j, core=core):
                hop_last(j, core).wait_send()

    out_copy.wait()


def body(n, features, centres, samples, counts, label_row, owner):
    rows = 2 * features.shape[0]
    images = label_row.shape[0]
    slots = samples.shape[1]
    held, width = centres.shape
    dma = pltpu.SemaphoreType.DMA
    vmem = pl.BlockSpec(memory_space=pltpu.VMEM)
    anywhere = pl.BlockSpec(memory_space=pl.ANY)
    feature_grad, centre_grad, loss_all = pl.pallas_call(
        functools.partial(kernel, n, rows, images, slots, held),
        out_shape=(
            jax.ShapeDtypeStruct(features.shape, f32),
            jax.ShapeDtypeStruct((slots, width), bf16),
            jax.ShapeDtypeStruct((1, images), f32),
        ),
        in_specs=[vmem, anywhere, vmem, pl.BlockSpec(memory_space=pltpu.SMEM), vmem, vmem],
        out_specs=(vmem, anywhere, vmem),
        scratch_shapes=[
            pltpu.VMEM((held, width), bf16),
            pltpu.VMEM((slots, width), bf16),
            pltpu.VMEM((slots, width), bf16),
            pltpu.VMEM((width, slots), bf16),
            pltpu.VMEM((slots, L), f32),
            pltpu.VMEM((images, L), f32),
            pltpu.VMEM((2, n, n, rows, H), bf16),
            pltpu.VMEM((images, width), bf16),
            pltpu.VMEM((2, images, H), f32),
            pltpu.VMEM((images, L), f32),
            pltpu.VMEM((images, slots), f32),
            pltpu.VMEM((images, slots), bf16),
            pltpu.VMEM((2, n, n, rows, H), f32),
            pltpu.VMEM((rows // 2, L), f32),
            pltpu.VMEM((2, 2, rows // 2, L), f32),
            pltpu.VMEM((2, images), f32),
            pltpu.VMEM((n, 2, images), f32),
            pltpu.VMEM((n, 2, images), f32),
            pltpu.VMEM((8, 2, images), f32),
            pltpu.VMEM((n, n, rows, H), bf16),
            pltpu.VMEM((n, n, rows, H), bf16),
            pltpu.VMEM((n - 1, n, rows, H), bf16),
            pltpu.VMEM((n, rows, H), f32),
            pltpu.VMEM((n - 1, n, rows, H), bf16),
            pltpu.VMEM((n, rows, H), f32),
            pltpu.VMEM((n - 1, rows, H), f32),
            pltpu.VMEM((2, 2, rows // 2, L), f32),
            pltpu.VMEM((4, rows // 2, L), f32),
            pltpu.VMEM((slots, width), bf16),
            dma(()), dma(()),
            dma((4,)), dma((4,)),
            dma((n - 1,)), dma((n - 1,)),
            dma((n - 1,)), dma((n - 1,)),
            dma((n,)), dma((n,)),
            dma((n - 1,)), dma((n - 1,)),
            dma((n - 1,)), dma((n - 1,)),
            dma((7,)), dma((7,)),
            dma((n,)), dma((n,)),
            dma((n - 1,)), dma((n - 1,)),
            dma((n - 1,)), dma((n - 1,)),
            dma((4,)), dma((4,)),
        ],
        compiler_params=pltpu.CompilerParams(
            collective_id=0, has_side_effects=True, vmem_limit_bytes=56 * 1024 * 1024
        ),
    )(features, centres, samples, counts, label_row[None], owner[None])
    own = features.shape[0]
    loss = lax.dynamic_slice_in_dim(loss_all[0], lax.axis_index("cls") * own, own, 0)
    return feature_grad, centre_grad[None], loss


def solution(mesh):
    n = math.isqrt(mesh.shape["cls"] // 2)
    return jax.shard_map(
        functools.partial(body, n),
        mesh=mesh,
        in_specs=(
            P("cls", "role"),
            P(("role", "cls"), None),
            P(("role", "cls"), None),
            P(("role", "cls")),
            P(),
            P(),
        ),
        out_specs=(P("cls", "role"), P(("role", "cls"), None, None), P("cls")),
        check_vma=False,
    )
```

time: 1210 us -> 84.5 us (0.07)
  blocking collectives: 877 us -> 0 us
  waiting for transfers between devices: 277 us -> 0 us
  Pallas kernels: 0 us -> 78.2 us
  other arithmetic: 15.3 us -> 0 us
  matrix products: 14.8 us -> 0 us
  between operations: 15.2 us -> 1.29 us
    psum x6 -> x0, blocking collectives: 869 us -> none  [the longest x1 255 us: body(): col_mean = lax.psum(jnp.sum(values, 0), 'cls') / images]
    unnamed x4 -> x0, waiting for transfers between devices: 189 us -> none
    pallas_call x0 -> x1, Pallas kernels: none -> 78.2 us  [body(): pl.pallas_call(functools.partial(kernel, n, rows, images, slots, held), o...]
    all_gather x1 -> x0, waiting for transfers between devices: 66.5 us -> none  [body(): gathered = lax.all_gather(widened, 'cls', axis=0, tiled=True)]
    reduce_scatter x1 -> x0, waiting for transfers between devices: 22 us -> none  [body(): lax.psum_scatter(full_grad, 'role', scatter_dimension=1, tiled=True)]
    dot_general x3 -> x0, matrix products: 14.8 us -> none  [the longest x1 7.42 us: body(): lax.dot_general(gathered, w_round, (((1,), (1,)), ((), ())), preferred_el...]
  transfers between devices with their start and end apart: 3 -> 0, of which waited for: 3 -> 0; matrix products, arithmetic and copies ran while one was open for 2% -> 0% of each run, Pallas kernels for 0% -> 0%
where the time goes in v1:
time: 84.5 us; the launch traced here: 84.2 us
  Pallas kernels  78.2 us (93%)
  local copies, waits for them, and re-layouts  4.75 us (6%)
  between operations  1.29 us (2%)
    pallas_call x1, Pallas kernels, body(): pl.pallas_call(functools.partial(kernel, n, rows, images, slots, held), o...  78.2 us
    unnamed x2, local copies, waits for them, and re-layouts  3.53 us

profile of v1, /device:TPU:1, one launch (start us, length us, event | category | flops | bytes accessed | tf_op | source)
XLA Modules:
  0.0 84.2 jit_solution(6871419029317018845)
XLA Ops:
  1.3 78.2 %shard_map.85 = (f32[8,128]{1,0:T(8,128)}, bf16[1024,512]{1,0:T(8,128)(2,1)}, f32[1,1024]{1,0:T(1,128)}) custom-call(bf16[8,128]{1,0:T(8,128)(2,1)} %feat_ref.1, bf16[3072,512]{1,0:T(8,128)(2,1)} %cen_hbm.1, s32[1,1024]{1,0:T(1,128)} %samp_ref.1, s32[1]{0:T(128)S(6)} %copy.11.count_ref, s32[1,1024]{1,0:T(1,128)} %bitcast.6, s32[1,1024]{1,0:T(1,128)} %bitcast.7), custom_call_target="tpu_custom_call" | custom-call | tf_op jit(solution)/shard_map/pallas_call | solution.py:450
  79.5 1.2 %dynamic-slice_bitcast_fusion = f32[8]{0:T(128)} fusion(f32[1,1024]{1,0:T(1,128)} %get-tuple-element.8, s32[]{:T(128)S(6)} %select_n.3), kind=kLoop, calls=%fused_computation | loop fusion | bytes 68 | tf_op jit(solution)/shard_map/dynamic_slice | solution.py:507
  80.7 1.3 %copy.12 = f32[8,128]{1,0:T(8,128)} copy(f32[8,128]{1,0:T(8,128)} %get-tuple-element.12) | data formatting | bytes 8192
  82.0 2.3 %copy.13 = bf16[1,1024,512]{2,1,0:T(8,128)(2,1)} copy(bf16[1,1024,512]{2,1,0:T(8,128)(2,1)} %bitcast.5) | data formatting | bytes 2097152

commit v2 on v0

v2 whole, which is shorter than its diff:
```python
import functools
import math

import jax
import jax.numpy as jnp
from jax import lax
from jax.experimental import pallas as pl
from jax.experimental.pallas import tpu as pltpu
from jax.sharding import PartitionSpec as P

logit_scale = 64.0
margin_cos = math.cos(0.5)
margin_sin = math.sin(0.5)
epsilon = 1e-05

MESH = pl.DeviceIdType.MESH
f32 = jnp.float32
bf16 = jnp.bfloat16
L = 128


def column(row):
    return jnp.transpose(jnp.broadcast_to(row, (L, L)))


def row_sum(block):
    return jnp.sum(jnp.transpose(block), axis=0, keepdims=True)


def margin_logit(cos):
    sine = jnp.sqrt(jnp.maximum(1.0 - cos * cos, 0.0))
    return logit_scale * (cos * margin_cos - sine * margin_sin)


def wide(block, width):
    return jnp.concatenate([block] * (width // L), axis=1)


def add_all(ref, count):
    terms = [ref[i] for i in range(count)]
    while len(terms) > 1:
        terms = [terms[i] + terms[i + 1] for i in range(0, len(terms), 2)]
    return terms[0]


def kernel(
    n, roles, rows, slots, held,
    feat_hbm, cen_hbm, samp_hbm, count_hbm, label_hbm, owner_hbm,
    fg_hbm, cg_hbm, loss_hbm,
    feat, samp_row, ints, count, cen, picked, wround, wtrans, winv, labels, xbuf, feats, normed, inorm,
    ebuf, posexp, qn, qw, gbuf, qbuf, a_src, a_recv, part1, part2, cos1, cos2, scale,
    part1_in, part2_in, cos1_in, cos2_in, fsend, drecv, csend, csum, crecv, asrc, arecv, cgbuf, fg, loss,
    in_sem, out_sem, s1_s, s1_r, s2_s, s2_r, d_s, d_r, p1, p2, q1, q2, ds_s, ds_r, r2, r1,
):
    x = lax.axis_index("role")
    c = lax.axis_index("cls")
    k = c % 2
    t = c // 2
    y = t // n
    z = t % n
    width = L * roles
    own = rows // 2
    per = n // 2
    images = n * n * rows
    m = n * rows
    a = y + (z - y) * k
    b = z + (y - z) * k
    step_a = 2 * n - (2 * n - 2) * k
    step_b = 2 + (2 * n - 2) * k
    other = c + 1 - 2 * k
    q = (y + z) % 2
    aq = y + (z - y) * q
    step_q = 2 * n - (2 * n - 2) * q
    parity = (b + k) % 2
    self_one = k == q

    def remote(src, dst, send, recv, device):
        return pltpu.make_async_remote_copy(
            src_ref=src, dst_ref=dst, send_sem=send, recv_sem=recv, device_id=device, device_id_type=MESH
        )

    def wait_bytes(ref, sem):
        pltpu.make_async_copy(ref, ref, sem).wait()

    def far(o, size):
        return min(o, size - o)

    plane = [(i, o) for i in range(roles) for o in range(n)][1:]
    plane = sorted(plane, key=lambda p: -(far(p[0], roles) + far(p[1], n)))
    peers = len(plane)
    near = [sorted(range(p, n, 2), key=lambda o: far(o, n)) for p in range(2)]

    def in_plane(i, o):
        return (x + i) % roles, c + ((b + o) % n - b) * step_b

    barrier = pltpu.get_barrier_semaphore()

    def signal(device):
        pl.semaphore_signal(barrier, inc=1, device_id=device, device_id_type=MESH)

    def unless(condition, fn, *args):
        pl.when(jnp.logical_not(condition))(functools.partial(fn, *args))

    for i, o in plane:
        signal(in_plane(i, o))
    for core in range(2):
        at, step = (y, 2 * n) if core == 0 else (z, 2)
        for o in range(1, n):
            signal((x, c - k + core + ((at + o) % n - at) * step))
    signal((x, other))
    target_one = [(x, c - k + q + ((aq + o) % n - aq) * step_q) for o in range(n)]
    source_one = {
        (i, core): (x, c - k + core + (2 * i + parity - a) * step_a) for i in range(per) for core in range(2)
    }

    def is_me(i, core):
        return jnp.logical_and(2 * i + parity == a, k == core)

    for o in range(1, n):
        signal(target_one[o])
    unless(self_one, signal, target_one[0])
    for key in source_one:
        unless(is_me(*key), signal, source_one[key])

    feat_copy = pltpu.make_async_copy(feat_hbm, feat, in_sem.at[0])
    centre_copy = pltpu.make_async_copy(cen_hbm, cen, in_sem.at[1])
    count_copy = pltpu.make_async_copy(count_hbm, count, in_sem.at[2])
    int_copies = [
        pltpu.make_async_copy(src, dst, in_sem.at[3 + i])
        for i, (src, dst) in enumerate(((samp_hbm, samp_row), (label_hbm, ints.at[0]), (owner_hbm, ints.at[1])))
    ]
    for copy in (feat_copy, *int_copies, count_copy, centre_copy):
        copy.start()
    feat_copy.wait()
    a_src[...] = feat[...].astype(f32)
    for copy in int_copies:
        copy.wait()
    count_copy.wait()
    pl.semaphore_wait(barrier, peers + 4 * n - 1 - 2 * self_one.astype(jnp.int32))

    def hop_one(o):
        e = near[o % 2].index((n - o) % n)
        return remote(a_src, a_recv.at[e, k], s1_s, s1_r.at[e], target_one[o])

    for o in sorted(range(1, n), key=lambda o: -far(o, n)):
        hop_one(o).start()
    unless(self_one, lambda: hop_one(0).start())

    @pl.when(self_one)
    def _():
        a_recv[0, k] = a_src[...]

    shard = x * (2 * n * n) + c
    label_eff = jnp.where(ints[1] == shard, ints[0], -1).astype(f32)
    for i in range(images // L):
        labels[i * L : (i + 1) * L, :] = column(label_eff[:, i * L : (i + 1) * L])
    slot = lax.broadcasted_iota(jnp.int32, (1, slots), 1)
    usable = slot < count[0, 0]
    slot_ids = jnp.where(usable, samp_row[...], -2).astype(f32)
    slot_bias = jnp.where(usable, 0.0, -1e30).astype(f32)
    centre_copy.wait()

    lane = lax.broadcasted_iota(jnp.int32, (L, L), 1).astype(f32)

    def pick(i, carry):
        at = pl.ds(pl.multiple_of(i * L, L), L)
        ids = column(samp_row[:, at].astype(f32))
        hot = [jnp.where(ids == lane + (j * L), 1.0, 0.0).astype(bf16) for j in range(held // L)]
        rows_f = jnp.dot(jnp.concatenate(hot, axis=1), cen[...], preferred_element_type=f32)
        picked[at, :] = rows_f.astype(bf16)
        inv = lax.rsqrt(jnp.sum(rows_f * rows_f, axis=1, keepdims=True) + epsilon)
        unit = rows_f * inv
        winv[at, :] = jnp.broadcast_to(inv, (L, L))
        wround[at, :] = unit.astype(bf16)
        wtrans[:, at] = jnp.transpose(unit).astype(bf16)
        return carry

    blocks = slots // L
    cuts = [blocks * i // 8 for i in (0, 2, 3, 4, 5, 6, 7, 8)]

    def pick_some(i):
        if cuts[i] < cuts[i + 1]:
            lax.fori_loop(cuts[i], cuts[i + 1], pick, 0)

    pick_some(0)

    def tile_place(e):
        at = (a + jnp.where(self_one, near[0][e], near[1][e])) % n
        ty, tz = at + (y - at) * k, z + (at - z) * k
        return ty // 2, ty % 2, tz // 2, tz % 2

    def distance(i, o):
        return far(i, roles) + far(o, n)

    distances = sorted({distance(i, o) for i, o in plane})

    def hop_two(e, i, o):
        part = xbuf.at[(x, *tile_place(e))]
        return remote(part, part, s2_s, s2_r.at[distances.index(distance(i, o))], in_plane(i, o))

    for e in range(per):
        if e == 0:

            @pl.when(self_one)
            def _():
                wait_bytes(a_recv.at[0, 0], s1_r.at[0])

            unless(self_one, lambda: wait_bytes(a_recv.at[0], s1_r.at[0]))
        else:
            wait_bytes(a_recv.at[e], s1_r.at[e])
        xbuf[(x, *tile_place(e))] = jnp.concatenate([a_recv[e, 0], a_recv[e, 1]], axis=0).astype(bf16)
        for i, o in plane:
            hop_two(e, i, o).start()

    def tiles(ref, core, role, at):
        if core == 0:
            return ref.at[role, :, at % 2, at // 2, at % 2]
        return ref.at[role, at // 2, at % 2, :, (at + 1) % 2]

    def hop_three(core, i, o):
        part = tiles(xbuf, core, (x + roles - i) % roles, (b + n - o) % n)
        return remote(part, part, d_s, d_r, (x, other))

    def cross_part(members):
        for core in range(2):

            @pl.when(k == core)
            def _(core=core):
                for i, o in members:
                    hop_three(core, i, o).start()

    cross_part([(0, 0)])
    for e, dist in enumerate(distances):
        pick_some(1 + e)
        members = [p for p in plane if distance(*p) == dist]
        wait_bytes(csend.at[pl.ds(0, len(members))], s2_r.at[e])
        cross_part(members)
    for e in range(1 + len(distances), len(cuts) - 1):
        pick_some(e)
    wait_bytes(drecv.at[:, :, 0], d_r)

    def part_of(i):
        return jnp.concatenate(
            [xbuf[r, i // 2, i % 2].reshape(m, L).astype(f32) for r in range(roles)], axis=1
        )

    zero = jnp.zeros((1, width), f32)
    mean = lax.fori_loop(0, n, lambda i, s: s + jnp.sum(part_of(i), axis=0, keepdims=True), zero) / images

    def add_squares(i, s):
        centred = part_of(i) - mean
        return s + jnp.sum(centred * centred, axis=0, keepdims=True)

    inv_std = lax.rsqrt(lax.fori_loop(0, n, add_squares, zero) / images + epsilon)

    first_lane = lax.broadcasted_iota(jnp.int32, (m, L), 1) == 0

    def forward(i):
        at = slice(i * m, (i + 1) * m)
        norm = (part_of(i) - mean) * inv_std
        inv = lax.rsqrt(jnp.sum(norm * norm, axis=1, keepdims=True) + epsilon)
        inorm[at, :] = jnp.broadcast_to(inv, (m, L))
        normed[at, :] = norm
        unit = (norm * inv).astype(bf16)
        feats[at, :] = unit
        cosine = jnp.dot(unit, wtrans[...], preferred_element_type=f32)
        label = labels[at, :]
        cos_pos = jnp.zeros((m, L), f32)
        sums = jnp.zeros((m, L), f32)
        for j in range(slots // L):
            lanes = slice(j * L, (j + 1) * L)
            hit = label == slot_ids[:, lanes]
            cos = cosine[:, lanes]
            term = jnp.where(hit, 0.0, jnp.exp(logit_scale * cos + slot_bias[:, lanes]))
            ebuf[at, lanes] = term
            sums += term
            cos_pos += jnp.where(hit, cos, 0.0)
        total = jnp.sum(cos_pos, axis=1, keepdims=True)
        pos_exp = jnp.broadcast_to(jnp.exp(margin_logit(total)), (m, L))
        posexp[at, :] = pos_exp
        sums += jnp.where(jnp.logical_and(first_lane, label >= 0.0), pos_exp, 0.0)
        part1[i : i + 1, :] = row_sum(sums)
        cos1[i : i + 1, :] = row_sum(cos_pos)

    for i in range(n):
        forward(i)

    def sum_one(src, dst, sems, i, o):
        return remote(src, dst.at[x * n + b], sems.at[0], sems.at[1], in_plane(i, o))

    def sum_two(src, dst, sems, core, o):
        device = (x, c - k + core + ((a + o) % n - a) * step_a)
        return remote(src, dst.at[k * n + a], sems.at[0], sems.at[1], device)

    def each_two(src, dst, sems, act):
        for core in range(2):
            for o in range(1, n):
                act(sum_two(src, dst, sems, core, o))
        act(remote(src, dst.at[k * n + a], sems.at[0], sems.at[1], (x, other)))

    def start_one(src, dst, sems):
        dst[x * n + b] = src[...]
        for i, o in plane:
            sum_one(src, dst, sems, i, o).start()

    def finish_one(src, dst, sems, total):
        wait_bytes(dst.at[pl.ds(0, peers)], sems.at[1])
        total[...] = add_all(dst, roles * n)

    def start_two(src, dst, sems):
        dst[k * n + a] = src[...]
        each_two(src, dst, sems, lambda copy: copy.start())

    def finish_two(src, dst, sems):
        wait_bytes(dst.at[pl.ds(0, 2 * n - 1)], sems.at[1])
        return add_all(dst, 2 * n)

    part_one = (part1, part1_in, p1)
    part_two = (part2, part2_in, p2)
    cos_one = (cos1, cos1_in, q1)
    cos_two = (cos2, cos2_in, q2)
    start_one(*part_one)
    start_one(*cos_one)

    def by_terms(i, carry):
        at = pl.ds(pl.multiple_of(i * m, m), m)
        label = labels[at, :]
        hits = jnp.concatenate(
            [
                jnp.where(label == slot_ids[:, j * L : (j + 1) * L], 1.0, 0.0).astype(bf16)
                for j in range(slots // L)
            ],
            axis=1,
        )
        left = jnp.concatenate([ebuf[at, :].astype(bf16), hits], axis=0)
        both = jnp.dot(left, wround[...], preferred_element_type=f32)
        inv = wide(inorm[at, :], width)
        unit = normed[at, :] * inv
        for out, term in ((qn, both[:m]), (qw, both[m:])):
            radial = jnp.sum(unit * term, axis=1, keepdims=True)
            out[at, :] = (term - unit * radial) * inv
        return carry

    lax.fori_loop(0, n * 5 // 8, by_terms, 0)

    finish_one(*part_one, part2)
    start_two(*part_two)

    lax.fori_loop(n * 5 // 8, n, by_terms, 0)

    finish_one(*cos_one, cos2)
    start_two(*cos_two)

    total = finish_two(*part_two)
    log_sum = jnp.log(total)
    scale[...] = logit_scale / total

    def factors(i, at):
        plain = column(scale[pl.ds(i, 1), :])
        return plain, (posexp[at, :] * plain - logit_scale).astype(bf16).astype(f32)

    shift, slope = zero, zero
    for i in range(n):
        at = slice(i * m, (i + 1) * m)
        plain, hit = factors(i, at)
        value = qn[at, :] * wide(plain, width) + qw[at, :] * wide(hit, width)
        qn[at, :] = value
        shift += jnp.sum(value, axis=0, keepdims=True)
        slope += jnp.sum(value * normed[at, :], axis=0, keepdims=True)
    shift, slope = shift / images, slope / images

    def finish(i, carry):
        at = pl.ds(pl.multiple_of(i * m, m), m)
        value = (qn[at, :] - shift - normed[at, :] * slope) * inv_std
        for r in range(roles):
            tile = value[:, r * L : (r + 1) * L].reshape(n // 2, 2, rows, L)
            qbuf[r, i // 2, i % 2] = tile
            fsend[r, i // 2, i % 2] = tile.astype(bf16)
        return carry

    lax.fori_loop(0, n, finish, 0)

    def cross(core, i):
        every = pl.ds(0, roles)
        return remote(tiles(fsend, 1 - core, every, i), tiles(drecv, 1 - core, every, i), ds_s, ds_r.at[i], (x, other))

    for core in range(2):

        @pl.when(k == core)
        def _(core=core):
            for i in range(n):
                cross(core, i).start()

    def reduce_two(e, i, o):
        return remote(csend.at[e], crecv.at[e], r2.at[0], r2.at[1], in_plane(i, o))

    for i in range(n):
        wait_bytes(tiles(drecv, 0, pl.ds(0, roles), 0), ds_r.at[i])
    for core in range(2):

        @pl.when(k == core)
        def _(core=core):
            def both(role, at):
                return tiles(qbuf, core, role, at)[...] + tiles(drecv, core, role, at)[...].astype(f32)

            for e, (i, o) in enumerate(plane):
                csend[e] = both((x + i) % roles, (b + o) % n).astype(bf16)
                reduce_two(e, i, o).start()
            csum[...] = both(x, b)

    def logit_grad(i, carry):
        at = pl.ds(pl.multiple_of(i * m, m), m)
        plain, hit = factors(i, at)
        label = labels[at, :]
        for j in range(slots // L):
            lanes = slice(j * L, (j + 1) * L)
            gbuf[at, lanes] = jnp.where(label == slot_ids[:, lanes], hit, ebuf[at, lanes] * plain).astype(bf16)
        return carry

    lax.fori_loop(0, n, logit_grad, 0)

    def by_centre(i, carry):
        at = pl.ds(pl.multiple_of(i * L, L), L)
        back = lax.dot_general(gbuf[:, at], feats[...], (((0,), (0,)), ((), ())), preferred_element_type=f32)
        inv = wide(winv[at, :], width)
        unit = picked[at, :].astype(f32) * inv
        radial = jnp.sum(unit * back, axis=1, keepdims=True)
        cgbuf[at, :] = ((back - unit * radial) * inv).astype(bf16)
        return carry

    lax.fori_loop(0, slots // L, by_centre, 0)
    cg_copy = pltpu.make_async_copy(cgbuf, cg_hbm, out_sem.at[0])
    cg_copy.start()

    losses = log_sum - margin_logit(finish_two(*cos_two))
    row = lax.broadcasted_iota(jnp.int32, (n, L), 0)
    losses = jnp.sum(jnp.where(row == y, losses, 0.0), axis=0, keepdims=True)
    losses = pltpu.roll(jnp.broadcast_to(losses, (8, L)), (L - z * rows - k * own) % L, 1)
    loss[...] = losses[0:1, :own]
    loss_copy = pltpu.make_async_copy(loss, loss_hbm, out_sem.at[1])
    loss_copy.start()

    wait_bytes(crecv, r2.at[1])
    total = csum[...]
    for e in range(peers):
        total += crecv[e].astype(f32)

    def reduce_one(i, core):
        return remote(asrc.at[i, core], arecv.at[a], r1.at[0], r1.at[1], source_one[i, core])

    for i, core in source_one:
        asrc[i, core] = total[i, core * own : (core + 1) * own, :]
        unless(is_me(i, core), lambda i, core: reduce_one(i, core).start(), i, core)

        @pl.when(is_me(i, core))
        def _(i=i, core=core):
            arecv[a] = asrc[i, core]

    @pl.when(self_one)
    def _():
        wait_bytes(arecv.at[pl.ds(0, n - 1)], r1.at[1])

    unless(self_one, lambda: wait_bytes(arecv, r1.at[1]))
    fg[...] = add_all(arecv, n)
    fg_copy = pltpu.make_async_copy(fg, fg_hbm, out_sem.at[2])
    fg_copy.start()

    @pl.when(self_one)
    def _():
        wait_bytes(arecv.at[pl.ds(0, n - 1)], s1_s)
        wait_bytes(arecv.at[pl.ds(0, n - 1)], r1.at[0])

    @pl.when(jnp.logical_not(self_one))
    def _():
        wait_bytes(arecv, s1_s)
        wait_bytes(arecv, r1.at[0])

    wait_bytes(csend, s2_s)
    wait_bytes(drecv.at[:, :, 0], d_s)
    wait_bytes(drecv.at[:, :, 0], ds_s)
    wait_bytes(csend, r2.at[0])
    for sems in (p1, q1):
        wait_bytes(part1_in.at[pl.ds(0, peers)], sems.at[0])
    for sems in (p2, q2):
        wait_bytes(part2_in.at[pl.ds(0, 2 * n - 1)], sems.at[0])
    cg_copy.wait()
    loss_copy.wait()
    fg_copy.wait()


def hand_on(fg_in, cg_in, loss_in, fg_out, cg_out, loss_out, fg, cg, loss, sem):
    parts = 4
    size = cg_in.shape[0] // parts
    pairs = [(fg_in, fg, fg_out), (loss_in, loss, loss_out)]
    pairs += [tuple(ref.at[pl.ds(i * size, size)] for ref in (cg_in, cg, cg_out)) for i in range(parts)]
    ins = [pltpu.make_async_copy(src, mid, sem.at[i]) for i, (src, mid, _) in enumerate(pairs)]
    outs = [pltpu.make_async_copy(mid, dst, sem.at[i]) for i, (_, mid, dst) in enumerate(pairs)]
    for copy in ins:
        copy.start()
    for copy, out in zip(ins, outs):
        copy.wait()
        out.start()
    for out in outs:
        out.wait()


def body(n, roles, features, centres, samples, counts, label_row, owner):
    own = features.shape[0]
    rows = 2 * own
    images = label_row.shape[0]
    slots = samples.shape[1]
    held, width = centres.shape
    per = n // 2
    peers = roles * n - 1
    distances = roles // 2 + n // 2
    tiles = (roles, per, 2, per, 2, rows, L)
    dma = pltpu.SemaphoreType.DMA
    anywhere = pl.BlockSpec(memory_space=pl.ANY)
    hbm = pl.BlockSpec(memory_space=pltpu.HBM)
    out_shape = (
        jax.ShapeDtypeStruct(features.shape, f32),
        jax.ShapeDtypeStruct((slots, width), bf16),
        jax.ShapeDtypeStruct((1, own), f32),
    )
    results = pl.pallas_call(
        functools.partial(kernel, n, roles, rows, slots, held),
        out_shape=out_shape,
        in_specs=[hbm] * 6,
        out_specs=(anywhere,) * 3,
        scratch_shapes=[
            pltpu.VMEM(features.shape, bf16),
            pltpu.VMEM((1, slots), jnp.int32),
            pltpu.VMEM((2, 1, images), jnp.int32),
            pltpu.SMEM((1, 1), jnp.int32),
            pltpu.VMEM((held, width), bf16),
            pltpu.VMEM((slots, width), bf16),
            pltpu.VMEM((slots, width), bf16),
            pltpu.VMEM((width, slots), bf16),
            pltpu.VMEM((slots, L), f32),
            pltpu.VMEM((images, L), f32),
            pltpu.VMEM(tiles, bf16),
            pltpu.VMEM((images, width), bf16),
            pltpu.VMEM((images, width), f32),
            pltpu.VMEM((images, L), f32),
            pltpu.VMEM((images, slots), f32),
            pltpu.VMEM((images, L), f32),
            pltpu.VMEM((images, width), f32),
            pltpu.VMEM((images, width), f32),
            pltpu.VMEM((images, slots), bf16),
            pltpu.VMEM(tiles, f32),
            pltpu.VMEM((own, L), f32),
            pltpu.VMEM((per, 2, own, L), f32),
            pltpu.VMEM((n, L), f32),
            pltpu.VMEM((n, L), f32),
            pltpu.VMEM((n, L), f32),
            pltpu.VMEM((n, L), f32),
            pltpu.VMEM((n, L), f32),
            pltpu.VMEM((roles * n, n, L), f32),
            pltpu.VMEM((2 * n, n, L), f32),
            pltpu.VMEM((roles * n, n, L), f32),
            pltpu.VMEM((2 * n, n, L), f32),
            pltpu.VMEM(tiles, bf16),
            pltpu.VMEM(tiles, bf16),
            pltpu.VMEM((peers, per, rows, L), bf16),
            pltpu.VMEM((per, rows, L), f32),
            pltpu.VMEM((peers, per, rows, L), bf16),
            pltpu.VMEM((per, 2, own, L), f32),
            pltpu.VMEM((n, own, L), f32),
            pltpu.VMEM((slots, width), bf16),
            pltpu.VMEM((own, L), f32),
            pltpu.VMEM((1, own), f32),
            dma((6,)), dma((3,)),
            dma(()), dma((per,)),
            dma(()), dma((distances,)),
            dma(()), dma(()),
            dma((2,)), dma((2,)), dma((2,)), dma((2,)),
            dma(()), dma((n,)),
            dma((2,)), dma((2,)),
        ],
        compiler_params=pltpu.CompilerParams(
            collective_id=0, has_side_effects=True, vmem_limit_bytes=56 * 1024 * 1024
        ),
    )(features, centres, samples, counts[None], label_row[None], owner[None])
    feature_grad, centre_grad, loss = pl.pallas_call(
        hand_on,
        out_shape=out_shape,
        in_specs=[anywhere] * 3,
        out_specs=(anywhere,) * 3,
        scratch_shapes=[
            pltpu.VMEM(features.shape, f32), pltpu.VMEM((slots, width), bf16), pltpu.VMEM((1, own), f32), dma((6,))
        ],
    )(*results)
    return feature_grad, centre_grad[None], loss[0]


def solution(mesh):
    n = math.isqrt(mesh.shape["cls"] // 2)
    return jax.shard_map(
        functools.partial(body, n, mesh.shape["role"]),
        mesh=mesh,
        in_specs=(
            P("cls", "role"),
            P(("role", "cls"), None),
            P(("role", "cls"), None),
            P(("role", "cls")),
            P(),
            P(),
        ),
        out_specs=(P("cls", "role"), P(("role", "cls"), None, None), P("cls")),
        check_vma=False,
    )
```

time: 1210 us -> 67.6 us (0.06)
  blocking collectives: 877 us -> 0 us
  waiting for transfers between devices: 277 us -> 0 us
  Pallas kernels: 0 us -> 66.2 us
  other arithmetic: 15.3 us -> 0 us
  matrix products: 14.8 us -> 0 us
  between operations: 15.2 us -> 1.29 us
  local copies, waits for them, and re-layouts: 12.9 us -> 0 us
    psum x6 -> x0, blocking collectives: 869 us -> none  [the longest x1 255 us: body(): col_mean = lax.psum(jnp.sum(values, 0), 'cls') / images]
    unnamed x4 -> x0, waiting for transfers between devices: 189 us -> none
    all_gather x1 -> x0, waiting for transfers between devices: 66.5 us -> none  [body(): gathered = lax.all_gather(widened, 'cls', axis=0, tiled=True)]
    pallas_call x0 -> x2, Pallas kernels: none -> 66.2 us  [the longest x1 64.2 us: body(): pl.pallas_call(functools.partial(kernel, n, roles, rows, slots, held), ou...]
    reduce_scatter x1 -> x0, waiting for transfers between devices: 22 us -> none  [body(): lax.psum_scatter(full_grad, 'role', scatter_dimension=1, tiled=True)]
    dot_general x3 -> x0, matrix products: 14.8 us -> none  [the longest x1 7.42 us: body(): lax.dot_general(gathered, w_round, (((1,), (1,)), ((), ())), preferred_el...]
  transfers between devices with their start and end apart: 3 -> 0, of which waited for: 3 -> 0; matrix products, arithmetic and copies ran while one was open for 2% -> 0% of each run, Pallas kernels for 0% -> 0%
where the time goes in v2:
time: 67.6 us; the launch traced here: 67.5 us
  Pallas kernels  66.2 us (98%)
  between operations  1.29 us (2%)
    pallas_call x1, Pallas kernels, body(): pl.pallas_call(functools.partial(kernel, n, roles, rows, slots, held), ou...  64.2 us
    pallas_call x1, Pallas kernels, body(): pl.pallas_call(hand_on, out_shape=out_shape, in_specs=[anywhere] * 3, out...  1.97 us

profile of v2, /device:TPU:1, one launch (start us, length us, event | category | flops | bytes accessed | tf_op | source)
XLA Modules:
  0.0 67.5 jit_solution(13336169980093509075)
XLA Ops:
  1.3 64.2 %shard_map.85 = (f32[8,128]{1,0:T(8,128)}, bf16[1024,512]{1,0:T(8,128)(2,1)}, f32[1,8]{1,0:T(1,128)}) custom-call(bf16[8,128]{1,0:T(8,128)(2,1)} %feat_hbm.1, bf16[3072,512]{1,0:T(8,128)(2,1)} %cen_hbm.1, s32[1,1024]{1,0:T(1,128)} %samp_hbm.1, s32[1,1]{1,0:T(1,128)} %bitcast.5.count_hbm, s32[1,1024]{1,0:T(1,128)} %bitcast.6, s32[1,1024]{1,0:T(1,128)} %bitcast.7), custom_call_target="tpu_custom_call" | custom-call | tf_op jit(solution)/shard_map/pallas_call | solution.py:525
  65.5 2.0 %shard_map.86 = (f32[8,128]{1,0:T(8,128)}, bf16[1024,512]{1,0:T(8,128)(2,1)}, f32[1,8]{1,0:T(1,128)}) custom-call(f32[8,128]{1,0:T(8,128)} %get-tuple-element.9.fg_in, bf16[1024,512]{1,0:T(8,128)(2,1)} %get-tuple-element.10.cg_in, f32[1,8]{1,0:T(1,128)} %get-tuple-element.11.loss_in), custom_call_target="tpu_custom_call" | custom-call | tf_op jit(solution)/shard_map/pallas_call | solution.py:584

commit v3 on v2

--- a/solution.py
+++ b/solution.py
@@ -46,11 +46,11 @@
 def kernel(
     n, roles, rows, slots, held,
     feat_hbm, cen_hbm, samp_hbm, count_hbm, label_hbm, owner_hbm,
-    fg_hbm, cg_hbm, loss_hbm,
+    fg, cgbuf, loss,
     feat, samp_row, ints, count, cen, picked, wround, wtrans, winv, labels, xbuf, feats, normed, inorm,
-    ebuf, posexp, qn, qw, gbuf, qbuf, a_src, a_recv, part1, part2, cos1, cos2, scale,
-    part1_in, part2_in, cos1_in, cos2_in, fsend, drecv, csend, csum, crecv, asrc, arecv, cgbuf, fg, loss,
-    in_sem, out_sem, s1_s, s1_r, s2_s, s2_r, d_s, d_r, p1, p2, q1, q2, ds_s, ds_r, r2, r1,
+    ebuf, posexp, qn, qw, gbuf, qbuf, a_src, a_recv, part1, part2, cos1, cos2, cosbuf, scale,
+    part1_in, part2_in, cos1_in, cos2_in, fsend, drecv, csend, csum, crecv, asrc, arecv,
+    in_sem, s1_s, s1_r, s2_s, s2_r, d_s, d_r, p1, p2, q1, q2, ds_s, ds_r, r2_s, r2_r, r1,
 ):
     x = lax.axis_index("role")
     c = lax.axis_index("cls")
@@ -176,7 +176,7 @@
         return carry
 
     blocks = slots // L
-    cuts = [blocks * i // 8 for i in (0, 2, 3, 4, 5, 6, 7, 8)]
+    cuts = [blocks * i // 8 for i in (0, 1, 3, 4, 5, 6, 7, 8)]
 
     def pick_some(i):
         if cuts[i] < cuts[i + 1]:
@@ -233,7 +233,7 @@
     for e, dist in enumerate(distances):
         pick_some(1 + e)
         members = [p for p in plane if distance(*p) == dist]
-        wait_bytes(csend.at[pl.ds(0, len(members))], s2_r.at[e])
+        wait_bytes(csend.at[:, pl.ds(0, len(members))], s2_r.at[e])
         cross_part(members)
     for e in range(1 + len(distances), len(cuts) - 1):
         pick_some(e)
@@ -280,7 +280,7 @@
         posexp[at, :] = pos_exp
         sums += jnp.where(jnp.logical_and(first_lane, label >= 0.0), pos_exp, 0.0)
         part1[i : i + 1, :] = row_sum(sums)
-        cos1[i : i + 1, :] = row_sum(cos_pos)
+        cosbuf[at, :] = cos_pos
 
     for i in range(n):
         forward(i)
@@ -320,6 +320,8 @@
     cos_one = (cos1, cos1_in, q1)
     cos_two = (cos2, cos2_in, q2)
     start_one(*part_one)
+    for i in range(n):
+        cos1[i : i + 1, :] = row_sum(cosbuf[i * m : (i + 1) * m, :])
     start_one(*cos_one)
 
     def by_terms(i, carry):
@@ -348,9 +350,6 @@
 
     lax.fori_loop(n * 5 // 8, n, by_terms, 0)
 
-    finish_one(*cos_one, cos2)
-    start_two(*cos_two)
-
     total = finish_two(*part_two)
     log_sum = jnp.log(total)
     scale[...] = logit_scale / total
@@ -369,44 +368,67 @@
         slope += jnp.sum(value * normed[at, :], axis=0, keepdims=True)
     shift, slope = shift / images, slope / images
 
-    def finish(i, carry):
-        at = pl.ds(pl.multiple_of(i * m, m), m)
-        value = (qn[at, :] - shift - normed[at, :] * slope) * inv_std
-        for r in range(roles):
-            tile = value[:, r * L : (r + 1) * L].reshape(n // 2, 2, rows, L)
-            qbuf[r, i // 2, i % 2] = tile
-            fsend[r, i // 2, i % 2] = tile.astype(bf16)
-        return carry
-
-    lax.fori_loop(0, n, finish, 0)
+    def finish(core, out):
+        def block(i, carry):
+            p = (i + core) % 2
+            for j in range(per):
+                at = pl.ds(pl.multiple_of(i * m + (2 * j + p) * rows, rows), rows)
+                value = (qn[at, :] - shift - normed[at, :] * slope) * inv_std
+                for r in range(roles):
+                    out[r, i // 2, i % 2, j, p] = value[:, r * L : (r + 1) * L].astype(out.dtype)
+            return carry
+
+        lax.fori_loop(0, n, block, 0)
+
+    finish(1 - k, fsend)
+
+    by_far = sorted(range(n), key=lambda o: -far(o, n))
 
     def cross(core, i):
         every = pl.ds(0, roles)
-        return remote(tiles(fsend, 1 - core, every, i), tiles(drecv, 1 - core, every, i), ds_s, ds_r.at[i], (x, other))
+        return remote(
+            tiles(fsend, 1 - core, every, i), tiles(drecv, 1 - core, every, i), ds_s, ds_r.at[i], (x, other)
+        )
 
     for core in range(2):
 
         @pl.when(k == core)
         def _(core=core):
-            for i in range(n):
-                cross(core, i).start()
-
-    def reduce_two(e, i, o):
-        return remote(csend.at[e], crecv.at[e], r2.at[0], r2.at[1], in_plane(i, o))
-
-    for i in range(n):
-        wait_bytes(tiles(drecv, 0, pl.ds(0, roles), 0), ds_r.at[i])
-    for core in range(2):
-
-        @pl.when(k == core)
-        def _(core=core):
-            def both(role, at):
-                return tiles(qbuf, core, role, at)[...] + tiles(drecv, core, role, at)[...].astype(f32)
-
-            for e, (i, o) in enumerate(plane):
-                csend[e] = both((x + i) % roles, (b + o) % n).astype(bf16)
-                reduce_two(e, i, o).start()
-            csum[...] = both(x, b)
+            for o in by_far:
+                cross(core, (a + o) % n).start()
+
+    finish(k, qbuf)
+
+    def tile_of(at, e):
+        return ((a + jnp.where((a + at + k) % 2 == 0, near[0][e], near[1][e])) % n) // 2
+
+    def reduce_two(e, f, i, o):
+        return remote(csend.at[e, f], crecv.at[e, f], r2_s, r2_r.at[e], in_plane(i, o))
+
+    arrived = set()
+
+    def cross_wait(o):
+        if o not in arrived:
+            arrived.add(o)
+            wait_bytes(tiles(drecv, 0, pl.ds(0, roles), 0), ds_r.at[(b + o) % n])
+
+    def both(e, role, at):
+        i = tile_of(at, e)
+        ay, by = i, at // 2
+        pa, pb = (at + k) % 2, at % 2
+        place = (role, ay + (by - ay) * k, pa + (pb - pa) * k, by + (ay - by) * k, pb + (pa - pb) * k)
+        return qbuf[place] + drecv[place].astype(f32)
+
+    for e in reversed(range(per)):
+        for f, (i, o) in enumerate(plane):
+            cross_wait(o)
+            csend[e, f] = both(e, (x + i) % roles, (b + o) % n).astype(bf16)
+            reduce_two(e, f, i, o).start()
+        cross_wait(0)
+        csum[e] = both(e, x, b)
+
+    finish_one(*cos_one, cos2)
+    start_two(*cos_two)
 
     def logit_grad(i, carry):
         at = pl.ds(pl.multiple_of(i * m, m), m)
@@ -429,32 +451,35 @@
         return carry
 
     lax.fori_loop(0, slots // L, by_centre, 0)
-    cg_copy = pltpu.make_async_copy(cgbuf, cg_hbm, out_sem.at[0])
-    cg_copy.start()
 
     losses = log_sum - margin_logit(finish_two(*cos_two))
     row = lax.broadcasted_iota(jnp.int32, (n, L), 0)
     losses = jnp.sum(jnp.where(row == y, losses, 0.0), axis=0, keepdims=True)
     losses = pltpu.roll(jnp.broadcast_to(losses, (8, L)), (L - z * rows - k * own) % L, 1)
     loss[...] = losses[0:1, :own]
-    loss_copy = pltpu.make_async_copy(loss, loss_hbm, out_sem.at[1])
-    loss_copy.start()
-
-    wait_bytes(crecv, r2.at[1])
-    total = csum[...]
-    for e in range(peers):
-        total += crecv[e].astype(f32)
-
-    def reduce_one(i, core):
-        return remote(asrc.at[i, core], arecv.at[a], r1.at[0], r1.at[1], source_one[i, core])
-
-    for i, core in source_one:
-        asrc[i, core] = total[i, core * own : (core + 1) * own, :]
-        unless(is_me(i, core), lambda i, core: reduce_one(i, core).start(), i, core)
-
-        @pl.when(is_me(i, core))
-        def _(i=i, core=core):
-            arecv[a] = asrc[i, core]
+
+    def reduce_one(e, core):
+        device = (x, c - k + core + ((a + jnp.where(self_one, near[0][e], near[1][e])) % n - a) * step_a)
+        return remote(asrc.at[e, core], arecv.at[a], r1.at[0], r1.at[1], device)
+
+    for e in reversed(range(per)):
+        wait_bytes(crecv.at[e], r2_r.at[e])
+        terms = [csum[e]] + [crecv[e, f].astype(f32) for f in range(peers)]
+        while len(terms) > 1:
+            terms = [terms[i] + terms[i + 1] for i in range(0, len(terms), 2)]
+        for core in range(2):
+            asrc[e, core] = terms[0][core * own : (core + 1) * own, :]
+        if e:
+            for core in range(2):
+                reduce_one(e, core).start()
+        else:
+            for core in range(2):
+                me = jnp.logical_and(self_one, k == core)
+                unless(me, lambda core: reduce_one(0, core).start(), core)
+
+                @pl.when(me)
+                def _(core=core):
+                    arecv[a] = asrc[0, core]
 
     @pl.when(self_one)
     def _():
@@ -462,8 +487,6 @@
 
     unless(self_one, lambda: wait_bytes(arecv, r1.at[1]))
     fg[...] = add_all(arecv, n)
-    fg_copy = pltpu.make_async_copy(fg, fg_hbm, out_sem.at[2])
-    fg_copy.start()
 
     @pl.when(self_one)
     def _():
@@ -478,30 +501,23 @@
     wait_bytes(csend, s2_s)
     wait_bytes(drecv.at[:, :, 0], d_s)
     wait_bytes(drecv.at[:, :, 0], ds_s)
-    wait_bytes(csend, r2.at[0])
+    wait_bytes(csend, r2_s)
     for sems in (p1, q1):
         wait_bytes(part1_in.at[pl.ds(0, peers)], sems.at[0])
     for sems in (p2, q2):
         wait_bytes(part2_in.at[pl.ds(0, 2 * n - 1)], sems.at[0])
-    cg_copy.wait()
-    loss_copy.wait()
-    fg_copy.wait()
-
-
-def hand_on(fg_in, cg_in, loss_in, fg_out, cg_out, loss_out, fg, cg, loss, sem):
-    parts = 4
+
+
+def hand_on(fg_in, cg_in, loss_in, fg_out, cg_out, loss_out, sem):
+    parts = 8
     size = cg_in.shape[0] // parts
-    pairs = [(fg_in, fg, fg_out), (loss_in, loss, loss_out)]
-    pairs += [tuple(ref.at[pl.ds(i * size, size)] for ref in (cg_in, cg, cg_out)) for i in range(parts)]
-    ins = [pltpu.make_async_copy(src, mid, sem.at[i]) for i, (src, mid, _) in enumerate(pairs)]
-    outs = [pltpu.make_async_copy(mid, dst, sem.at[i]) for i, (_, mid, dst) in enumerate(pairs)]
-    for copy in ins:
+    pairs = [(fg_in, fg_out), (loss_in, loss_out)]
+    pairs += [tuple(ref.at[pl.ds(i * size, size)] for ref in (cg_in, cg_out)) for i in range(parts)]
+    copies = [pltpu.make_async_copy(src, dst, sem.at[i]) for i, (src, dst) in enumerate(pairs)]
+    for copy in copies:
         copy.start()
-    for copy, out in zip(ins, outs):
+    for copy in copies:
         copy.wait()
-        out.start()
-    for out in outs:
-        out.wait()
 
 
 def body(n, roles, features, centres, samples, counts, label_row, owner):
@@ -516,6 +532,7 @@
     tiles = (roles, per, 2, per, 2, rows, L)
     dma = pltpu.SemaphoreType.DMA
     anywhere = pl.BlockSpec(memory_space=pl.ANY)
+    vmem = pl.BlockSpec(memory_space=pltpu.VMEM)
     hbm = pl.BlockSpec(memory_space=pltpu.HBM)
     out_shape = (
         jax.ShapeDtypeStruct(features.shape, f32),
@@ -524,9 +541,9 @@
     )
     results = pl.pallas_call(
         functools.partial(kernel, n, roles, rows, slots, held),
-        out_shape=out_shape,
+        out_shape=tuple(pltpu.VMEM(s.shape, s.dtype) for s in out_shape),
         in_specs=[hbm] * 6,
-        out_specs=(anywhere,) * 3,
+        out_specs=(vmem,) * 3,
         scratch_shapes=[
             pltpu.VMEM(features.shape, bf16),
             pltpu.VMEM((1, slots), jnp.int32),
@@ -554,6 +571,7 @@
             pltpu.VMEM((n, L), f32),
             pltpu.VMEM((n, L), f32),
             pltpu.VMEM((n, L), f32),
+            pltpu.VMEM((images, L), f32),
             pltpu.VMEM((n, L), f32),
             pltpu.VMEM((roles * n, n, L), f32),
             pltpu.VMEM((2 * n, n, L), f32),
@@ -561,21 +579,19 @@
             pltpu.VMEM((2 * n, n, L), f32),
             pltpu.VMEM(tiles, bf16),
             pltpu.VMEM(tiles, bf16),
-            pltpu.VMEM((peers, per, rows, L), bf16),
+            pltpu.VMEM((per, peers, rows, L), bf16),
             pltpu.VMEM((per, rows, L), f32),
-            pltpu.VMEM((peers, per, rows, L), bf16),
+            pltpu.VMEM((per, peers, rows, L), bf16),
             pltpu.VMEM((per, 2, own, L), f32),
             pltpu.VMEM((n, own, L), f32),
-            pltpu.VMEM((slots, width), bf16),
-            pltpu.VMEM((own, L), f32),
-            pltpu.VMEM((1, own), f32),
-            dma((6,)), dma((3,)),
+            dma((6,)),
             dma(()), dma((per,)),
             dma(()), dma((distances,)),
             dma(()), dma(()),
             dma((2,)), dma((2,)), dma((2,)), dma((2,)),
             dma(()), dma((n,)),
-            dma((2,)), dma((2,)),
+            dma(()), dma((per,)),
+            dma((2,)),
         ],
         compiler_params=pltpu.CompilerParams(
             collective_id=0, has_side_effects=True, vmem_limit_bytes=56 * 1024 * 1024
@@ -584,12 +600,10 @@
     feature_grad, centre_grad, loss = pl.pallas_call(
         hand_on,
         out_shape=out_shape,
-        in_specs=[anywhere] * 3,
+        in_specs=[vmem] * 3,
         out_specs=(anywhere,) * 3,
-        scratch_shapes=[
-            pltpu.VMEM(features.shape, f32), pltpu.VMEM((slots, width), bf16), pltpu.VMEM((1, own), f32), dma((6,))
-        ],
-    )(*results)
+        scratch_shapes=[dma((10,))],
+    )(*(pltpu.with_memory_space_constraint(r, pltpu.VMEM) for r in results))
     return feature_grad, centre_grad[None], loss[0]
 
 

time: 67.6 us -> 65.9 us (0.975)
  Pallas kernels: 66.2 us -> 64.3 us
    pallas_call x1, Pallas kernels: 64.2 us -> 63.3 us  [body(): pl.pallas_call(functools.partial(kernel, n, roles, rows, slots, held), ou...]
    pallas_call x1, Pallas kernels: 1.97 us -> 1.05 us  [body(): pl.pallas_call(hand_on, out_shape=out_shape, in_specs=[vmem] * 3, out_spe...]
where the time goes in v3:
time: 65.9 us; the launch traced here: 65.8 us
  Pallas kernels  64.3 us (98%)
  between operations  1.45 us (2%)
    pallas_call x1, Pallas kernels, body(): pl.pallas_call(functools.partial(kernel, n, roles, rows, slots, held), ou...  63.3 us

profile of v3, /device:TPU:1, one launch (start us, length us, event | category | flops | bytes accessed | tf_op | source)
XLA Modules:
  0.0 65.8 jit_solution(9674629088405579969)
XLA Ops:
  1.3 63.3 %shard_map.85 = (f32[8,128]{1,0:T(8,128)S(1)}, bf16[1024,512]{1,0:T(8,128)(2,1)S(1)}, f32[1,8]{1,0:T(1,128)S(1)}) custom-call(bf16[8,128]{1,0:T(8,128)(2,1)} %feat_hbm.1, bf16[3072,512]{1,0:T(8,128)(2,1)} %cen_hbm.1, s32[1,1024]{1,0:T(1,128)} %samp_hbm.1, s32[1,1]{1,0:T(1,128)} %bitcast.5.count_hbm, s32[1,1024]{1,0:T(1,128)} %bitcast.6, s32[1,1024]{1,0:T(1,128)} %bitcast.7), custom_call_target="tpu_custom_call" | custom-call | tf_op jit(solution)/shard_map/pallas_call | solution.py:542
  64.5 1.1 %shard_map.86 = (f32[8,128]{1,0:T(8,128)}, bf16[1024,512]{1,0:T(8,128)(2,1)}, f32[1,8]{1,0:T(1,128)}) custom-call(f32[8,128]{1,0:T(8,128)S(1)} %get-tuple-element.9.fg_in, bf16[1024,512]{1,0:T(8,128)(2,1)S(1)} %get-tuple-element.10.cg_in, f32[1,8]{1,0:T(1,128)S(1)} %get-tuple-element.11.loss_in), custom_call_target="tpu_custom_call" | custom-call | tf_op jit(solution)/shard_map/pallas_call | solution.py:600

commit v4 on v3

--- a/solution.py
+++ b/solution.py
@@ -244,14 +244,13 @@
             [xbuf[r, i // 2, i % 2].reshape(m, L).astype(f32) for r in range(roles)], axis=1
         )
 
-    zero = jnp.zeros((1, width), f32)
-    mean = lax.fori_loop(0, n, lambda i, s: s + jnp.sum(part_of(i), axis=0, keepdims=True), zero) / images
-
-    def add_squares(i, s):
-        centred = part_of(i) - mean
-        return s + jnp.sum(centred * centred, axis=0, keepdims=True)
-
-    inv_std = lax.rsqrt(lax.fori_loop(0, n, add_squares, zero) / images + epsilon)
+    def column_sums(blocks):
+        total = functools.reduce(lambda u, v: u + v, [jnp.sum(v.reshape(m // 8, 8, width), axis=0) for v in blocks])
+        return jnp.sum(total, axis=0, keepdims=True)
+
+    mean = column_sums(part_of(i) for i in range(n)) / images
+    centred = (part_of(i) - mean for i in range(n))
+    inv_std = lax.rsqrt(column_sums(v * v for v in centred) / images + epsilon)
 
     first_lane = lax.broadcasted_iota(jnp.int32, (m, L), 1) == 0
 
@@ -294,7 +293,7 @@
 
     def each_two(src, dst, sems, act):
         for core in range(2):
-            for o in range(1, n):
+            for o in sorted(range(1, n), key=lambda o: -far(o, n)):
                 act(sum_two(src, dst, sems, core, o))
         act(remote(src, dst.at[k * n + a], sems.at[0], sems.at[1], (x, other)))
 
@@ -358,15 +357,15 @@
         plain = column(scale[pl.ds(i, 1), :])
         return plain, (posexp[at, :] * plain - logit_scale).astype(bf16).astype(f32)
 
-    shift, slope = zero, zero
+    values = []
     for i in range(n):
         at = slice(i * m, (i + 1) * m)
         plain, hit = factors(i, at)
         value = qn[at, :] * wide(plain, width) + qw[at, :] * wide(hit, width)
         qn[at, :] = value
-        shift += jnp.sum(value, axis=0, keepdims=True)
-        slope += jnp.sum(value * normed[at, :], axis=0, keepdims=True)
-    shift, slope = shift / images, slope / images
+        fold = [jnp.sum(v.reshape(m // 8, 8, width), axis=0) for v in (value, value * normed[at, :])]
+        values = [u + v for u, v in zip(values, fold)] if values else fold
+    shift, slope = (jnp.sum(v, axis=0, keepdims=True) / images for v in values)
 
     def finish(core, out):
         def block(i, carry):
@@ -378,7 +377,7 @@
                     out[r, i // 2, i % 2, j, p] = value[:, r * L : (r + 1) * L].astype(out.dtype)
             return carry
 
-        lax.fori_loop(0, n, block, 0)
+        lax.fori_loop(0, n, block, 0, unroll=4 if n % 4 == 0 else 1)
 
     finish(1 - k, fsend)
 

time: 65.9 us -> 65.5 us (level)
  no operation moved by 1% of the time
where the time goes in v4:
time: 65.5 us; the launch traced here: 65.4 us
  Pallas kernels  63.9 us (98%)
  between operations  1.45 us (2%)
    pallas_call x1, Pallas kernels, body(): pl.pallas_call(functools.partial(kernel, n, roles, rows, slots, held), ou...  62.9 us

profile of v4, /device:TPU:1, one launch (start us, length us, event | category | flops | bytes accessed | tf_op | source)
XLA Modules:
  0.0 65.4 jit_solution(4344717209061900866)
XLA Ops:
  1.3 62.9 %shard_map.85 = (f32[8,128]{1,0:T(8,128)S(1)}, bf16[1024,512]{1,0:T(8,128)(2,1)S(1)}, f32[1,8]{1,0:T(1,128)S(1)}) custom-call(bf16[8,128]{1,0:T(8,128)(2,1)} %feat_hbm.1, bf16[3072,512]{1,0:T(8,128)(2,1)} %cen_hbm.1, s32[1,1024]{1,0:T(1,128)} %samp_hbm.1, s32[1,1]{1,0:T(1,128)} %bitcast.5.count_hbm, s32[1,1024]{1,0:T(1,128)} %bitcast.6, s32[1,1024]{1,0:T(1,128)} %bitcast.7), custom_call_target="tpu_custom_call" | custom-call | tf_op jit(solution)/shard_map/pallas_call | solution.py:541
  64.2 1.1 %shard_map.86 = (f32[8,128]{1,0:T(8,128)}, bf16[1024,512]{1,0:T(8,128)(2,1)}, f32[1,8]{1,0:T(1,128)}) custom-call(f32[8,128]{1,0:T(8,128)S(1)} %get-tuple-element.9.fg_in, bf16[1024,512]{1,0:T(8,128)(2,1)S(1)} %get-tuple-element.10.cg_in, f32[1,8]{1,0:T(1,128)S(1)} %get-tuple-element.11.loss_in), custom_call_target="tpu_custom_call" | custom-call | tf_op jit(solution)/shard_map/pallas_call | solution.py:599

commit v5 on v4

--- a/solution.py
+++ b/solution.py
@@ -93,6 +93,16 @@
     def in_plane(i, o):
         return (x + i) % roles, c + ((b + o) % n - b) * step_b
 
+    feat_copy = pltpu.make_async_copy(feat_hbm, feat, in_sem.at[0])
+    centre_copy = pltpu.make_async_copy(cen_hbm, cen, in_sem.at[1])
+    count_copy = pltpu.make_async_copy(count_hbm, count, in_sem.at[2])
+    int_copies = [
+        pltpu.make_async_copy(src, dst, in_sem.at[3 + i])
+        for i, (src, dst) in enumerate(((samp_hbm, samp_row), (label_hbm, ints.at[0]), (owner_hbm, ints.at[1])))
+    ]
+    for copy in (feat_copy, *int_copies, count_copy, centre_copy):
+        copy.start()
+
     barrier = pltpu.get_barrier_semaphore()
 
     def signal(device):
@@ -122,34 +132,25 @@
     for key in source_one:
         unless(is_me(*key), signal, source_one[key])
 
-    feat_copy = pltpu.make_async_copy(feat_hbm, feat, in_sem.at[0])
-    centre_copy = pltpu.make_async_copy(cen_hbm, cen, in_sem.at[1])
-    count_copy = pltpu.make_async_copy(count_hbm, count, in_sem.at[2])
-    int_copies = [
-        pltpu.make_async_copy(src, dst, in_sem.at[3 + i])
-        for i, (src, dst) in enumerate(((samp_hbm, samp_row), (label_hbm, ints.at[0]), (owner_hbm, ints.at[1])))
-    ]
-    for copy in (feat_copy, *int_copies, count_copy, centre_copy):
-        copy.start()
     feat_copy.wait()
     a_src[...] = feat[...].astype(f32)
+    pl.semaphore_wait(barrier, peers + 4 * n - 1 - 2 * self_one.astype(jnp.int32))
+
+    def hop_one(o):
+        e = near[o % 2].index((n - o) % n)
+        return remote(a_src, a_recv.at[e, k], s1_s, s1_r.at[e], target_one[o])
+
+    for o in sorted(range(1, n), key=lambda o: -far(o, n)):
+        hop_one(o).start()
+    unless(self_one, lambda: hop_one(0).start())
+
+    @pl.when(self_one)
+    def _():
+        a_recv[0, k] = a_src[...]
+
     for copy in int_copies:
         copy.wait()
     count_copy.wait()
-    pl.semaphore_wait(barrier, peers + 4 * n - 1 - 2 * self_one.astype(jnp.int32))
-
-    def hop_one(o):
-        e = near[o % 2].index((n - o) % n)
-        return remote(a_src, a_recv.at[e, k], s1_s, s1_r.at[e], target_one[o])
-
-    for o in sorted(range(1, n), key=lambda o: -far(o, n)):
-        hop_one(o).start()
-    unless(self_one, lambda: hop_one(0).start())
-
-    @pl.when(self_one)
-    def _():
-        a_recv[0, k] = a_src[...]
-
     shard = x * (2 * n * n) + c
     label_eff = jnp.where(ints[1] == shard, ints[0], -1).astype(f32)
     for i in range(images // L):

time: 65.5 us -> 65.5 us (level)
  no operation moved by 1% of the time
where the time goes in v5:
time: 65.5 us; the launch traced here: 65.4 us
  Pallas kernels  63.9 us (98%)
  between operations  1.45 us (2%)
    pallas_call x1, Pallas kernels, body(): pl.pallas_call(functools.partial(kernel, n, roles, rows, slots, held), ou...  62.9 us

profile of v5, /device:TPU:1, one launch (start us, length us, event | category | flops | bytes accessed | tf_op | source)
XLA Modules:
  0.0 65.4 jit_solution(8055976135113982182)
XLA Ops:
  1.3 62.9 %shard_map.85 = (f32[8,128]{1,0:T(8,128)S(1)}, bf16[1024,512]{1,0:T(8,128)(2,1)S(1)}, f32[1,8]{1,0:T(1,128)S(1)}) custom-call(bf16[8,128]{1,0:T(8,128)(2,1)} %feat_hbm.1, bf16[3072,512]{1,0:T(8,128)(2,1)} %cen_hbm.1, s32[1,1024]{1,0:T(1,128)} %samp_hbm.1, s32[1,1]{1,0:T(1,128)} %bitcast.5.count_hbm, s32[1,1024]{1,0:T(1,128)} %bitcast.6, s32[1,1024]{1,0:T(1,128)} %bitcast.7), custom_call_target="tpu_custom_call" | custom-call | tf_op jit(solution)/shard_map/pallas_call | solution.py:542
  64.1 1.1 %shard_map.86 = (f32[8,128]{1,0:T(8,128)}, bf16[1024,512]{1,0:T(8,128)(2,1)}, f32[1,8]{1,0:T(1,128)}) custom-call(f32[8,128]{1,0:T(8,128)S(1)} %get-tuple-element.9.fg_in, bf16[1024,512]{1,0:T(8,128)(2,1)S(1)} %get-tuple-element.10.cg_in, f32[1,8]{1,0:T(1,128)S(1)} %get-tuple-element.11.loss_in), custom_call_target="tpu_custom_call" | custom-call | tf_op jit(solution)/shard_map/pallas_call | solution.py:600
